TPU v7x, 512 devices: a whole 4x8x8 slice. The times are simulated.
512 devices in a mesh: acq: 16 (over y, core), az: 32 (over x, z).
Axes of the slice: x: 4, y: 8, z: 8, core: 2. Of those that a mesh axis runs over, the one named last changes fastest.
Arguments:
- complex_slabs: bfloat16 [96, 2, 320, 2560], P('acq', None, 'az'), may hold values from -1250 to 1250
- secondaries: int32 [96, 10], P('acq'), may hold values from 1 to 95, as said below
- pair_counts: int32 [96], P('acq'), may hold values from 0 to 10, as said below
- phase_screens: float32 [96, 64, 128], P(None, 'az'), may hold values from -3.140625 to 3.140625
Outputs:
- screen_gradient: float32 [96, 64, 128], P('acq', 'az')
- pair_misfit: float32 [96, 64, 128], P('acq', 'az')
Inputs may be any that keep to these rules, and one draw needn't show every extreme that they name: `secondaries`: for every acquisition a, the first pair_counts[a] entries of row a are distinct acquisitions from a + 1 to a + 12; the remaining entries are ignored. pair_counts[a] <= min(10, 95 - a).
All inputs are finite; a program needn't handle non-finite values.
Results may differ from a plain program's by a relative error of at most 0.0003.
Values may be sent and summed in bfloat16 or wider, within the bound.
A program may use at most 128 MiB of HBM per device.

v0:
```python
import functools

import jax
import jax.numpy as jnp
import numpy as np
from jax import lax
from jax.experimental import pallas as pl
from jax.experimental.pallas import tpu as pltpu
from jax.sharding import PartitionSpec as P

EPSILON = 1e-6
MESH = pl.DeviceIdType.MESH
F32, BF16, I32 = jnp.float32, jnp.bfloat16, jnp.int32

ACQ = 6
OWN = 12
QUARTERS = 4
TILES = 5
GROUP = 2 * QUARTERS * ACQ
HALF = QUARTERS * ACQ
TOP, MID, RIM = 3 * GROUP, 5 * GROUP, 2 * GROUP


WIDE = TILES * 128


def gather_matrix():
    row, col = np.arange(WIDE)[:, None], np.arange(512)[None, :]
    tile, lane = row // 128, row % 128
    combine = np.logical_and(lane // 8 == col // 32, 6 * tile + lane % 8 == col % 32)
    sums = row // 20 == np.arange(128)[None, :] % 32
    return jnp.asarray(np.concatenate([combine, sums], axis=1), BF16)


def slot_of(a):
    return a // ACQ * 8 + a % ACQ


def iota(shape, dim):
    return lax.broadcasted_iota(I32, shape, dim)


def kernel(
    chips, slabs,
    x_hbm, sec_hbm, cnt_hbm, screens_hbm, gather_hbm,
    grad_ref, misfit_ref,
    xbuf, secs, cnts, screens, gather, spread, send, own, oth, ownf, masked, acc, raw, red, cross, power,
    mytab, owntab, othtab, mypow, othpow, phi, trig, turn, sums, msg_own, msg_oth, fin_own, fin_oth,
    load_sem, send_sem, rim_send, oth_recv, own_recv, rim_recv, small_send, small_recv,
):
    me = lax.axis_index("acq")
    az = lax.axis_index("az")
    y, core = me // 2, me % 2
    up, down = jnp.minimum(y + 1, chips - 1), jnp.maximum(y - 1, 0)
    az_next, az_prev = jnp.minimum(az + 1, slabs - 1), jnp.maximum(az - 1, 0)
    has_up, has_down = y < chips - 1, y > 0
    has_next, has_prev = az < slabs - 1, az > 0
    side = jnp.where(core == 0, up, down)
    has_side = jnp.logical_or(jnp.logical_and(core == 0, has_up), jnp.logical_and(core == 1, has_down))
    has_rim = jnp.logical_and(core == 0, has_prev)
    both = jnp.logical_and

    loads = [pltpu.make_async_copy(x_hbm.at[pl.ds(3 * i, 3)], xbuf.at[pl.ds(3 * i, 3)], load_sem.at[i]) for i in range(4)]
    loads += [
        pltpu.make_async_copy(sec_hbm, secs, load_sem.at[4]),
        pltpu.make_async_copy(cnt_hbm, cnts, load_sem.at[5]),
        pltpu.make_async_copy(screens_hbm.at[pl.ds(OWN * y, OWN)], screens.at[0], load_sem.at[6]),
        pltpu.make_async_copy(screens_hbm.at[pl.ds(OWN * side, OWN)], screens.at[1], load_sem.at[7]),
        pltpu.make_async_copy(gather_hbm, gather, load_sem.at[8]),
    ]
    for load in loads:
        load.start()

    fin_oth[...] = jnp.zeros_like(fin_oth)
    othtab[...] = jnp.full((2, 8, 128), -1, I32)

    barrier = pltpu.get_barrier_semaphore()

    def greet(a, z):
        pl.semaphore_signal(barrier, inc=1, device_id=(a, z), device_id_type=MESH)

    greet(2 * y + 1 - core, az)

    @pl.when(has_up)
    def _():
        for c in range(2):
            greet(2 * up + c, az)

    @pl.when(has_down)
    def _():
        for c in range(2):
            greet(2 * down + c, az)

    @pl.when(has_rim)
    def _():
        for c in range(2):
            greet(2 * y + c, az_prev)

        @pl.when(has_up)
        def _():
            for c in range(2):
                greet(2 * up + c, az_prev)

    def flag(condition):
        return jnp.where(condition, 1, 0)

    expected = 1 + 2 * flag(has_up) + 2 * flag(has_down) + flag(has_next) + flag(both(has_next, has_down))

    @pl.when(both(core == 0, jnp.logical_not(has_prev)))
    def _():
        own[:, :, 0:RIM, :] = jnp.zeros((2, TILES, RIM, 128), BF16)
        oth[:, :, 0:RIM, :] = jnp.zeros((2, TILES, RIM, 128), BF16)

    @pl.when(jnp.logical_not(has_side))
    def _():
        oth[...] = jnp.zeros_like(oth)

    loads[4].wait()
    loads[5].wait()
    mytab[...] = jnp.full((8, 128), -1, I32)
    mytab[0:ACQ, 0:10] = secs[...]
    slots = jnp.zeros((8, 128), I32)
    for i in range(ACQ):
        slots = jnp.where(iota((8, 128), 0) == i, cnts[i], slots)
    mytab[...] = jnp.where(iota((8, 128), 1) < slots, mytab[...], -1)
    owntab[core] = mytab[...]

    def small(k, src, dst, a, sem):
        return pltpu.make_async_remote_copy(
            src_ref=src, dst_ref=dst, send_sem=small_send.at[k], recv_sem=small_recv.at[sem],
            device_id=(a, az), device_id_type=MESH,
        )

    def wide(t, k, first, rows, buffer, start, a, sem):
        return pltpu.make_async_remote_copy(
            src_ref=send.at[t, pl.ds(first, rows)],
            dst_ref=buffer.at[core, t, pl.ds(start, rows)],
            send_sem=send_sem.at[t, k], recv_sem=sem,
            device_id=(a, az), device_id_type=MESH,
        )

    def to_down(t):
        return wide(t, 0, 0, TOP, oth, RIM, 2 * down, oth_recv.at[t, core])

    def to_up(t):
        return wide(t, 1, TOP, MID, oth, 0, 2 * up + 1, oth_recv.at[t, core])

    def to_core1(t):
        return wide(t, 2, TOP, MID, own, 0, 2 * y + 1, own_recv.at[t])

    def to_core0(t):
        return wide(t, 2, 0, TOP, own, RIM, 2 * y, own_recv.at[t])

    def rim_copy(k, buffer, a):
        return pltpu.make_async_remote_copy(
            src_ref=send.at[:, pl.ds(TOP + MID, RIM)],
            dst_ref=buffer.at[core, :, pl.ds(0, RIM)],
            send_sem=rim_send.at[k], recv_sem=rim_recv.at[k, core],
            device_id=(a, az_next), device_id_type=MESH,
        )

    def unpack(t, first, rows):
        for q in range(QUARTERS):
            lanes = pl.ds(pl.multiple_of(640 * q + 128 * t, 128), 128)
            for ac in range(2 * ACQ):
                start = (q * 2 * ACQ + ac) * 16 + first
                spread[start : start + rows, :] = xbuf[ac, first : first + rows, lanes].astype(F32)

    def pick(t, first, last):
        for r in range(first, last):
            parts = [spread[pl.ds(16 * c + r, HALF, stride=32), :] for c in range(2)]
            send[t, r * GROUP : (r + 1) * GROUP, :] = jnp.concatenate(parts, axis=0).astype(BF16)

    for i in range(4):
        loads[i].wait()

    def rim_tile(t, carry):
        unpack(t, 8, 2)
        pick(t, 8, 10)
        return carry

    lax.fori_loop(0, TILES, rim_tile, 0)
    pl.semaphore_wait(barrier, expected)

    @pl.when(has_next)
    def _():
        rim_copy(0, own, 2 * y).start()

        @pl.when(has_down)
        def _():
            rim_copy(1, oth, 2 * down).start()

    def main_tile(t, carry):
        unpack(t, 0, 8)
        pick(t, 0, 8)

        @pl.when(has_down)
        def _():
            to_down(t).start()

        @pl.when(has_up)
        def _():
            to_up(t).start()

        @pl.when(core == 0)
        def _():
            to_core1(t).start()
            own[0, t, RIM:, :] = send[t, 0:TOP, :]

        @pl.when(core == 1)
        def _():
            to_core0(t).start()
            own[1, t] = send[t, TOP : TOP + MID, :]

        return carry

    lax.fori_loop(0, TILES, main_tile, 0)

    tab_chip = small(0, mytab, owntab.at[core], 2 * y + 1 - core, 0)
    tab_chip.start()

    def tab_up(c):
        return small(1, mytab, othtab.at[c], 2 * up + 1, 1 + c)

    @pl.when(has_up)
    def _():
        tab_up(core).start()

    quarter = (iota((ACQ, 384), 1) >> 3) & 3

    def expand(t, first, last):
        column = iota((16, 128), 1) + 128 * t
        mask = jnp.where((((column * 3277) >> 16) - 6 * t) == (iota((16, 128), 0) & 7), 1.0, 0.0).astype(BF16)

        def step(k, carry):
            lanes = pl.ds(pl.multiple_of(128 * k, 128), 128)
            for c in range(2):
                for a in range(OWN):
                    for q in range(0, QUARTERS, 2):
                        source = k * GROUP + (HALF * c + ACQ * q + a % ACQ)
                        low = jnp.broadcast_to(ownf[a // ACQ, pl.ds(source, 1), :], (8, 128))
                        high = jnp.broadcast_to(ownf[a // ACQ, pl.ds(source + ACQ, 1), :], (8, 128))
                        start = 384 * c + 32 * a + 8 * q
                        masked[t, start : start + 16, lanes] = jnp.concatenate([low, high], axis=0).astype(BF16) * mask
            return carry

        lax.fori_loop(first, last, step, 0)

    def products(t, buffer, first, last):
        blocks = []
        for b in range(2):
            rows = [buffer[b, t, k * GROUP : (k + 1) * GROUP, :] for k in range(first, last)]
            blocks.append(jnp.concatenate(rows, axis=1))
        out = lax.dot_general(
            jnp.concatenate(blocks, axis=0), masked[t, :, 128 * first : 128 * last],
            (((1,), (1,)), ((), ())), preferred_element_type=F32,
        )
        real, imag = [], []
        for b in range(2):
            p, q = out[GROUP * b : GROUP * b + HALF], out[GROUP * b + HALF : GROUP * (b + 1)]
            real.append(p[:, :384] + q[:, 384:])
            imag.append(p[:, 384:] - q[:, :384])
        return jnp.concatenate(real + imag, axis=0)

    def squares(t, first, last):
        parts = []
        for b in range(2):
            total = None
            for k in range(first, last):
                v = oth[b, t, k * GROUP : (k + 1) * GROUP, :].astype(F32)
                term = v[:HALF] * v[:HALF] + v[HALF:] * v[HALF:]
                total = term if total is None else total + term
            parts.append(total)
        return jnp.concatenate(parts, axis=0)

    def own_tile(t, carry):
        @pl.when(core == 0)
        def _():
            to_core0(t).wait_recv()

        @pl.when(core == 1)
        def _():
            to_core1(t).wait_recv()

        for b in range(2):
            ownf[b, RIM:, :] = own[b, t, RIM:, :].astype(F32)
        expand(t, 2, 5)
        acc[0, t] = products(t, own, 2, 5)
        return carry

    lax.fori_loop(0, TILES, own_tile, 0)

    loads[6].wait()
    loads[7].wait()
    phi[...] = jnp.zeros_like(phi)
    for s in range(2):
        rows = screens[s]
        picked = jnp.where(core == 0, rows[:, 0, :], rows[:, 1, :])
        phi[16 * s : 16 * s + ACQ, :] = picked[0:ACQ]
        phi[16 * s + 8 : 16 * s + 8 + ACQ, :] = picked[ACQ:OWN]
    trig[0] = jnp.cos(phi[...])
    trig[1] = jnp.sin(phi[...])

    tab_chip.wait_recv()

    @pl.when(both(core == 1, has_down))
    def _():
        for c in range(2):
            tab_up(c).wait_recv()

    slot = iota((16, 128), 0)
    real_slot = (slot & 7) < ACQ
    member = (slot >> 3) * ACQ + (slot & 7)
    own_index = jnp.where(real_slot, OWN * y + member, -9)
    oth_index = jnp.where(real_slot, OWN * (y + 1) + member, -9)
    other_table = othtab[...].reshape(16, 128)
    for a in range(OWN):
        k = slot_of(a)
        cos_a, sin_a = trig[0, k : k + 1, :], trig[1, k : k + 1, :]
        line = owntab[a // ACQ, a % ACQ : a % ACQ + 1, :]
        theirs = jnp.where(other_table == OWN * y + a, 1.0, 0.0)
        hits = (
            jnp.where(line == own_index, 1.0, 0.0),
            jnp.where(core == 0, jnp.where(line == oth_index, 1.0, 0.0), theirs),
        )
        for s in range(2):
            w = jnp.sum(hits[s], axis=1, keepdims=True)
            cos_b, sin_b = trig[0, 16 * s : 16 * s + 16, :], trig[1, 16 * s : 16 * s + 16, :]
            turn[s, a, 0] = w * (cos_a * cos_b + sin_a * sin_b)
            turn[s, a, 1] = w * (sin_a * cos_b - cos_a * sin_b)
            turn[s, a, 2] = jnp.broadcast_to(w, (16, 128))

    def other_tile(t, carry):
        @pl.when(both(core == 0, has_up))
        def _():
            for b in range(2):
                wide(t, 0, 0, TOP, oth, RIM, me, oth_recv.at[t, b]).wait_recv()

        @pl.when(both(core == 1, has_down))
        def _():
            for b in range(2):
                wide(t, 1, TOP, MID, oth, 0, me, oth_recv.at[t, b]).wait_recv()

        acc[1, t] = products(t, oth, 2, 5)
        power[t] = squares(t, 2, 5)
        return carry

    lax.fori_loop(0, TILES, other_tile, 0)

    @pl.when(has_rim)
    def _():
        for b in range(2):
            pltpu.make_async_remote_copy(
                src_ref=send.at[:, pl.ds(TOP + MID, RIM)], dst_ref=own.at[b, :, pl.ds(0, RIM)],
                send_sem=rim_send.at[0], recv_sem=rim_recv.at[0, b], device_id=(me, az), device_id_type=MESH,
            ).wait_recv()

        @pl.when(has_up)
        def _():
            for b in range(2):
                pltpu.make_async_remote_copy(
                    src_ref=send.at[:, pl.ds(TOP + MID, RIM)], dst_ref=oth.at[b, :, pl.ds(0, RIM)],
                    send_sem=rim_send.at[1], recv_sem=rim_recv.at[1, b], device_id=(me, az), device_id_type=MESH,
                ).wait_recv()

    red[...] = jnp.zeros_like(red)

    def rim_rows(t, carry):
        for b in range(2):
            ownf[b, 0:RIM, :] = own[b, t, 0:RIM, :].astype(F32)
        expand(t, 0, 2)
        for s, buffer in enumerate((own, oth)):
            raw[s] = products(t, buffer, 0, 2) + acc[s, t]
            for g in range(4):
                v = [raw[s, HALF * g + ACQ * q : HALF * g + ACQ * (q + 1), :] for q in range(QUARTERS)]
                low = jnp.where(quarter == 0, v[0], v[1])
                high = jnp.where(quarter == 2, v[2], v[3])
                red[s, t, 8 * g : 8 * g + ACQ, :] = jnp.where(quarter < 2, low, high)
        power[t] += squares(t, 0, 2)
        return carry

    lax.fori_loop(0, TILES, rim_rows, 0)

    def split(v):
        high = v.astype(BF16)
        return [high, (v - high.astype(F32)).astype(BF16)]

    loads[8].wait()
    summed = jnp.concatenate(split(jnp.concatenate([power[t] for t in range(TILES)], axis=1)), axis=0)
    summed = jnp.dot(summed, gather[:, 512:], preferred_element_type=F32)
    power[0] = summed[0:48] + summed[48:96]
    othpow[...] = jnp.ones_like(othpow)
    cell_quarter = iota((ACQ, 128), 1) >> 5
    for b in range(2):
        v = [power[0, HALF * b + ACQ * q : HALF * b + ACQ * (q + 1), :] for q in range(QUARTERS)]
        low = jnp.where(cell_quarter == 0, v[0], v[1])
        high = jnp.where(cell_quarter == 2, v[2], v[3])
        othpow[8 * b : 8 * b + ACQ, :] = jnp.where(cell_quarter < 2, low, high)

    for s in range(2):
        stack = []
        for g in range(3):
            stack += split(jnp.concatenate([red[s, t, :, 128 * g : 128 * (g + 1)] for t in range(TILES)], axis=1))
        out = jnp.dot(jnp.concatenate(stack, axis=0), gather[:, :512], preferred_element_type=F32)
        for g in range(3):
            cross[s, g] = out[64 * g : 64 * g + 32] + out[64 * g + 32 : 64 * g + 64]

    mypow[...] = jnp.ones_like(mypow)
    for a in range(OWN):
        k = slot_of(a)
        mypow[k : k + 1, :] = cross[0, a // 4, k : k + 1, 128 * (a % 4) : 128 * (a % 4 + 1)]

    first = jnp.where(core == 0, 1.0, 0.0).astype(F32)
    sums[...] = jnp.zeros_like(sums)
    gain = [jnp.zeros((16, 128), F32), jnp.zeros((16, 128), F32)]
    loss = jnp.zeros((16, 128), F32)
    for a in range(OWN):
        k = slot_of(a)
        slopes, misses = [], []
        for s, powers in enumerate((mypow[...], othpow[...])):
            lanes = slice(128 * (a % 4), 128 * (a % 4 + 1))
            real, imag = cross[s, a // 4, 0:16, lanes], cross[s, a // 4, 16:32, lanes]
            norm = lax.rsqrt(mypow[k : k + 1, :] * powers + EPSILON)
            cosine, sine = turn[s, a, 0], turn[s, a, 1]
            slope = norm * (imag * cosine - real * sine)
            gain[s] += slope
            slopes.append(slope)
            misses.append(turn[s, a, 2] - norm * (real * cosine + imag * sine))
        loss += misses[1]
        sums[0, k : k + 1, :] = -jnp.sum(slopes[0] + slopes[1], axis=0, keepdims=True)
        sums[1, k : k + 1, :] = jnp.sum(misses[0] + first * misses[1], axis=0, keepdims=True)
    sums[0] += gain[0]
    for b in range(2):
        for f in range(2):
            msg_own[b, 8 * f : 8 * f + 8, :] = sums[f, 8 * b : 8 * b + 8, :]
        msg_oth[b, 0:8, :] = gain[1][8 * b : 8 * b + 8]
        msg_oth[b, 8:16, :] = (1.0 - first) * loss[8 * b : 8 * b + 8]
    fin_chip = small(2, msg_own.at[1 - core], fin_own.at[core], 2 * y + 1 - core, 3)
    fin_chip.start()

    def fin_side(b):
        return small(3 + b, msg_oth.at[b], fin_oth.at[core], 2 * side + b, 4 + core)

    @pl.when(has_side)
    def _():
        for b in range(2):
            fin_side(b).start()

    fin_own[core] = msg_own[core]
    fin_chip.wait_recv()

    @pl.when(has_down)
    def _():
        small(3, msg_oth.at[0], fin_oth.at[0], me, 4).wait_recv()

    @pl.when(has_up)
    def _():
        small(3, msg_oth.at[1], fin_oth.at[1], me, 5).wait_recv()

    for j in range(2):
        total = fin_own[j] + fin_oth[j]
        grad_ref[:, j, :] = total[0:ACQ]
        misfit_ref[:, j, :] = total[8 : 8 + ACQ]

    def drain(t, carry):
        @pl.when(has_down)
        def _():
            to_down(t).wait_send()

        @pl.when(has_up)
        def _():
            to_up(t).wait_send()

        @pl.when(core == 0)
        def _():
            to_core1(t).wait_send()

        @pl.when(core == 1)
        def _():
            to_core0(t).wait_send()

        return carry

    lax.fori_loop(0, TILES, drain, 0)

    @pl.when(has_next)
    def _():
        rim_copy(0, own, 2 * y).wait_send()

        @pl.when(has_down)
        def _():
            rim_copy(1, oth, 2 * down).wait_send()

    tab_chip.wait_send()

    @pl.when(has_up)
    def _():
        tab_up(core).wait_send()

    fin_chip.wait_send()

    @pl.when(has_side)
    def _():
        for b in range(2):
            fin_side(b).wait_send()


def local(chips, slabs, complex_slabs, secondaries, pair_counts, phase_screens):
    rows, columns = complex_slabs.shape[2:]
    x = complex_slabs.reshape(2 * ACQ, rows, columns)
    vmem = pl.BlockSpec(memory_space=pltpu.VMEM)
    hbm = pl.BlockSpec(memory_space=pltpu.HBM)
    out = jax.ShapeDtypeStruct((ACQ, 2, 128), F32)
    return pl.pallas_call(
        functools.partial(kernel, chips, slabs),
        out_shape=(out, out),
        in_specs=[hbm] * 5,
        out_specs=(vmem, vmem),
        scratch_shapes=[
            pltpu.VMEM((2 * ACQ, rows, columns), BF16),
            pltpu.VMEM(secondaries.shape, I32),
            pltpu.SMEM(pair_counts.shape, I32),
            pltpu.VMEM((2, OWN, 2, 128), F32),
            pltpu.VMEM((WIDE, 640), BF16),
            pltpu.VMEM((2 * ACQ * QUARTERS * 16, 128), F32),
            pltpu.VMEM((TILES, 10 * GROUP, 128), BF16),
            pltpu.VMEM((2, TILES, 5 * GROUP, 128), BF16),
            pltpu.VMEM((2, TILES, 5 * GROUP, 128), BF16),
            pltpu.VMEM((2, 5 * GROUP, 128), F32),
            pltpu.VMEM((TILES, 64 * OWN, WIDE), BF16),
            pltpu.VMEM((2, TILES, 96, 32 * OWN), F32),
            pltpu.VMEM((2, 96, 32 * OWN), F32),
            pltpu.VMEM((2, TILES, 32, 32 * OWN), F32),
            pltpu.VMEM((2, 3, 32, 512), F32),
            pltpu.VMEM((TILES, 48, 128), F32),
            pltpu.VMEM((8, 128), I32),
            pltpu.VMEM((2, 8, 128), I32),
            pltpu.VMEM((2, 8, 128), I32),
            pltpu.VMEM((16, 128), F32),
            pltpu.VMEM((16, 128), F32),
            pltpu.VMEM((32, 128), F32),
            pltpu.VMEM((2, 32, 128), F32),
            pltpu.VMEM((2, OWN, 3, 16, 128), F32),
            pltpu.VMEM((2, 16, 128), F32),
            pltpu.VMEM((2, 16, 128), F32),
            pltpu.VMEM((2, 16, 128), F32),
            pltpu.VMEM((2, 16, 128), F32),
            pltpu.VMEM((2, 16, 128), F32),
            pltpu.SemaphoreType.DMA((9,)),
            pltpu.SemaphoreType.DMA((TILES, 3)),
            pltpu.SemaphoreType.DMA((2,)),
            pltpu.SemaphoreType.DMA((TILES, 2)),
            pltpu.SemaphoreType.DMA((TILES,)),
            pltpu.SemaphoreType.DMA((2, 2)),
            pltpu.SemaphoreType.DMA((5,)),
            pltpu.SemaphoreType.DMA((6,)),
        ],
        compiler_params=pltpu.CompilerParams(
            collective_id=0, has_side_effects=True, vmem_limit_bytes=40 * 1024 * 1024
        ),
    )(x, secondaries, pair_counts, phase_screens, gather_matrix())


def solution(mesh):
    return jax.shard_map(
        functools.partial(local, mesh.shape["acq"] // 2, mesh.shape["az"]),
        mesh=mesh,
        in_specs=(P("acq", None, "az", None), P("acq", None), P("acq"), P(None, "az", None)),
        out_specs=(P("acq", "az", None), P("acq", "az", None)),
        check_vma=False,
    )
```

profile of v0, /device:TPU:39, one launch (start us, length us, event | category | flops | bytes accessed | tf_op | source)
XLA Modules:
  0.0 30.2 jit_solution(2755385339509632583)
XLA Ops:
  0.6 0.0 copy-start
  0.6 0.0 copy-start.1
  0.7 0.0 copy-start.2
  0.7 1.3 %copy.7 = bf16[6,2,10,2560]{3,2,1,0:T(8,128)(2,1)S(1)} copy(bf16[6,2,10,2560]{3,1,2,0:T(2,128)(2,1)} %param.5) | data formatting | bytes 1228800 | tf_op args[0]
  1.9 0.0 copy-start.3
  2.0 0.0 copy-done
  2.0 0.0 copy-done.1
  2.0 0.0 copy-done.2
  2.0 0.6 %copy-done.3 = s32[6]{0:T(128)S(1)} copy-done((s32[6]{0:T(128)S(1)}, s32[6]{0:T(128)}, u32[]{:S(2)}) %copy-start.3) | copy-done | bytes 48
  2.6 26.4 %shard_map.68 = (f32[6,2,128]{2,1,0:T(2,128)S(1)}, f32[6,2,128]{2,1,0:T(2,128)S(1)}) custom-call(bf16[12,10,2560]{2,1,0:T(8,128)(2,1)S(1)} %bitcast.1, s32[6,10]{1,0:T(8,128)S(1)} %copy-done.2, s32[6]{0:T(128)S(1)} %copy-done.3, f32[96,2,128]{2,1,0:T(2,128)S(1)} %copy-done.1, bf16[640,640]{1,0:T(8,128)(2,1)S(1)} %copy-done), custom_call_target="tpu_custom_call" | custom-call | tf_op jit(solution)/shard_map/pallas_call | solution.py:514
  29.0 0.6 %copy.10 = f32[6,2,128]{2,1,0:T(2,128)} copy(f32[6,2,128]{2,1,0:T(2,128)S(1)} %get-tuple-element.4) | data formatting | bytes 12288
  29.6 0.6 %copy.11 = f32[6,2,128]{2,1,0:T(2,128)} copy(f32[6,2,128]{2,1,0:T(2,128)S(1)} %get-tuple-element.5) | data formatting | bytes 12288
Async XLA Ops:
  0.6 1.3 %copy-start = (bf16[640,640]{1,0:T(8,128)(2,1)S(1)}, bf16[640,640]{1,0:T(8,128)(2,1)}, u32[]{:S(2)}) copy-start(bf16[640,640]{1,0:T(8,128)(2,1)} %constant.2.clone.gather_hbm) | copy-start | bytes 2457604
  0.6 1.3 %copy-start.1 = (f32[96,2,128]{2,1,0:T(2,128)S(1)}, f32[96,2,128]{2,1,0:T(2,128)}, u32[]{:S(2)}) copy-start(f32[96,2,128]{2,1,0:T(2,128)} %screens_hbm.1) | copy-start | bytes 294916
  0.7 1.3 %copy-start.2 = (s32[6,10]{1,0:T(8,128)S(1)}, s32[6,10]{1,0:T(8,128)}, u32[]{:S(2)}) copy-start(s32[6,10]{1,0:T(8,128)} %sec_hbm.1) | copy-start | bytes 724
  1.9 0.7 %copy-start.3 = (s32[6]{0:T(128)S(1)}, s32[6]{0:T(128)}, u32[]{:S(2)}) copy-start(s32[6]{0:T(128)} %cnt_hbm.1) | copy-start | bytes 76
where the time goes:
time: 30.4 us; the launch traced here: 30.2 us
  Pallas kernels  26.4 us (87%)
  local copies, waits for them, and re-layouts  3.11 us (10%)
  between operations  0.7 us (2%)
    pallas_call x1, Pallas kernels, local(): pl.pallas_call(functools.partial(kernel, chips, slabs), out_shape=(out, o...  26.4 us
    unnamed x11, local copies, waits for them, and re-layouts  3.11 us

commit v1 on v0

v1 whole, which is shorter than its diff:
```python
import functools

import jax
import jax.numpy as jnp
from jax import lax
from jax.experimental import pallas as pl
from jax.experimental.pallas import tpu as pltpu
from jax.sharding import PartitionSpec as P

EPSILON = 1e-6
MESH = pl.DeviceIdType.MESH
F32, BF16, I32 = jnp.float32, jnp.bfloat16, jnp.int32

ACQ = 6
OWN = 12
QUARTERS, TILES, QUARTER = 4, 5, 640
TOP, MID, RIM = 3, 5, 2


def iota(shape, dim):
    return lax.broadcasted_iota(I32, shape, dim)


def kernel(
    chips, slabs,
    x_hbm, sec_hbm, cnt_hbm, screens_hbm,
    grad_ref, misfit_ref,
    secs, cnts, screens, own, oth, ownf, othf, masked, acc, turned, square, power,
    mytab, owntab, othtab, partners, mypow, othpow, phi, trig, turn, sums, other_sums, msg_own, msg_oth, fin_own, fin_oth,
    load_sem, local_sem, send_sem, rim_send, oth_recv, own_recv, rim_recv, small_send, small_recv,
):
    me = lax.axis_index("acq")
    az = lax.axis_index("az")
    y, core = me // 2, me % 2
    up, down = jnp.minimum(y + 1, chips - 1), jnp.maximum(y - 1, 0)
    az_next, az_prev = jnp.minimum(az + 1, slabs - 1), jnp.maximum(az - 1, 0)
    has_up, has_down = y < chips - 1, y > 0
    has_next, has_prev = az < slabs - 1, az > 0
    side = jnp.where(core == 0, up, down)
    has_side = jnp.logical_or(jnp.logical_and(core == 0, has_up), jnp.logical_and(core == 1, has_down))
    has_rim = jnp.logical_and(core == 0, has_prev)
    both = jnp.logical_and

    loads = [
        pltpu.make_async_copy(sec_hbm, secs, load_sem.at[0]),
        pltpu.make_async_copy(cnt_hbm, cnts, load_sem.at[1]),
        pltpu.make_async_copy(screens_hbm.at[pl.ds(OWN * y, OWN)], screens.at[0], load_sem.at[2]),
        pltpu.make_async_copy(screens_hbm.at[pl.ds(OWN * side, OWN)], screens.at[1], load_sem.at[3]),
    ]
    for load in loads:
        load.start()

    def columns(q):
        return pl.ds(pl.multiple_of(QUARTER * q, 128), QUARTER)

    def local_top(q):
        return pltpu.make_async_copy(
            x_hbm.at[:, pl.ds(0, TOP), :, columns(q)], own.at[0, :, pl.ds(RIM, TOP), :, columns(q)], local_sem.at[q]
        )

    def local_mid(q):
        return pltpu.make_async_copy(
            x_hbm.at[:, pl.ds(TOP, MID), :, columns(q)], own.at[1, :, :, :, columns(q)], local_sem.at[q]
        )

    @pl.when(core == 0)
    def _():
        for q in range(QUARTERS):
            local_top(q).start()

    @pl.when(core == 1)
    def _():
        for q in range(QUARTERS):
            local_mid(q).start()

    fin_oth[...] = jnp.zeros_like(fin_oth)
    msg_own[...] = jnp.zeros_like(msg_own)
    msg_oth[...] = jnp.zeros_like(msg_oth)
    othtab[...] = jnp.full((2, 8, 128), -1, I32)

    barrier = pltpu.get_barrier_semaphore()

    def greet(a, z):
        pl.semaphore_signal(barrier, inc=1, device_id=(a, z), device_id_type=MESH)

    greet(2 * y + 1 - core, az)

    @pl.when(has_up)
    def _():
        for c in range(2):
            greet(2 * up + c, az)

    @pl.when(has_down)
    def _():
        for c in range(2):
            greet(2 * down + c, az)

    @pl.when(has_rim)
    def _():
        for c in range(2):
            greet(2 * y + c, az_prev)

        @pl.when(has_up)
        def _():
            for c in range(2):
                greet(2 * up + c, az_prev)

    def flag(condition):
        return jnp.where(condition, 1, 0)

    expected = 1 + 2 * flag(has_up) + 2 * flag(has_down) + flag(has_next) + flag(both(has_next, has_down))

    @pl.when(both(core == 0, jnp.logical_not(has_prev)))
    def _():
        own[:, :, 0:RIM] = jnp.zeros((2, ACQ, RIM, 2, QUARTERS * QUARTER), BF16)
        oth[:, :, 0:RIM] = jnp.zeros((2, ACQ, RIM, 2, QUARTERS * QUARTER), BF16)

    @pl.when(jnp.logical_not(has_side))
    def _():
        oth[...] = jnp.zeros_like(oth)

    loads[0].wait()
    loads[1].wait()
    mytab[...] = jnp.full((8, 128), -1, I32)
    mytab[0:ACQ, 0:10] = secs[...]
    slots = jnp.zeros((8, 128), I32)
    for i in range(ACQ):
        slots = jnp.where(iota((8, 128), 0) == i, cnts[i], slots)
    mytab[...] = jnp.where(iota((8, 128), 1) < slots, mytab[...], -1)
    owntab[core] = mytab[...]

    def small(k, src, dst, a, sem):
        return pltpu.make_async_remote_copy(
            src_ref=src, dst_ref=dst, send_sem=small_send.at[k], recv_sem=small_recv.at[sem],
            device_id=(a, az), device_id_type=MESH,
        )

    def wide(q, k, first, rows, buffer, start, a, sem):
        return pltpu.make_async_remote_copy(
            src_ref=x_hbm.at[:, pl.ds(first, rows), :, columns(q)],
            dst_ref=buffer.at[core, :, pl.ds(start, rows), :, columns(q)],
            send_sem=send_sem.at[q, k], recv_sem=sem,
            device_id=(a, az), device_id_type=MESH,
        )

    def to_down(q):
        return wide(q, 0, 0, TOP, oth, RIM, 2 * down, oth_recv.at[q, core])

    def to_up(q):
        return wide(q, 1, TOP, MID, oth, 0, 2 * up + 1, oth_recv.at[q, core])

    def to_core1(q):
        return wide(q, 2, TOP, MID, own, 0, 2 * y + 1, own_recv.at[q])

    def to_core0(q):
        return wide(q, 2, 0, TOP, own, RIM, 2 * y, own_recv.at[q])

    def rim_copy(k, block, buffer, a, z):
        return pltpu.make_async_remote_copy(
            src_ref=x_hbm.at[:, pl.ds(TOP + MID, RIM)],
            dst_ref=buffer.at[block, :, pl.ds(0, RIM)],
            send_sem=rim_send.at[k], recv_sem=rim_recv.at[k, block],
            device_id=(a, z), device_id_type=MESH,
        )

    pl.semaphore_wait(barrier, expected)

    @pl.when(has_next)
    def _():
        rim_copy(0, core, own, 2 * y, az_next).start()

        @pl.when(has_down)
        def _():
            rim_copy(1, core, oth, 2 * down, az_next).start()

    def start_wide(q, carry):
        @pl.when(core == 0)
        def _():
            to_core1(q).start()

        @pl.when(core == 1)
        def _():
            to_core0(q).start()

        @pl.when(has_down)
        def _():
            to_down(q).start()

        @pl.when(has_up)
        def _():
            to_up(q).start()

        return carry

    lax.fori_loop(0, QUARTERS, start_wide, 0)

    tab_chip = small(0, mytab, owntab.at[core], 2 * y + 1 - core, 0)
    tab_chip.start()

    def tab_up(c):
        return small(1, mytab, othtab.at[c], 2 * up + 1, 1 + c)

    @pl.when(has_up)
    def _():
        tab_up(core).start()

    def lay(buffer, rows, q, first, last):
        for r in range(first, last):
            for a in range(OWN):
                v = buffer[a // ACQ, a % ACQ, r, :, columns(q)].astype(F32)
                for t in range(TILES):
                    rows[r, q, pl.ds(2 * OWN * t + a, 2, stride=OWN), :] = v[:, 128 * t : 128 * (t + 1)]

    def cell_mask(t):
        column = iota((16, 128), 1) + 128 * t
        slot = ((column * 3277) >> 16) - 6 * t
        return jnp.where(slot == (iota((16, 128), 0) & 7), 1.0, 0.0).astype(BF16)

    masks = [cell_mask(t) for t in range(TILES)]

    def expand(q, t, first, last):
        for r in range(first, last):
            for c in range(2):
                start = 256 * r + 128 * c
                for a in range(0, OWN, 2):
                    source = 2 * OWN * t + OWN * c + a
                    low = jnp.broadcast_to(ownf[r, q, source : source + 1, :], (8, 128))
                    high = jnp.broadcast_to(ownf[r, q, source + 1 : source + 2, :], (8, 128))
                    block = jnp.concatenate([low, high], axis=0).astype(BF16) * masks[t]
                    masked[q, t, 8 * a : 8 * a + 16, start : start + 128] = block

    def planes(rows, q, t, r):
        start = 2 * OWN * t
        return rows[r, q, start : start + 16, :], rows[r, q, start + OWN : start + OWN + 16, :]

    def data(rows, q, t, first, last):
        real, imag = [], []
        for r in range(first, last):
            p, v = planes(rows, q, t, r)
            real += [p, v]
            imag += [-v, p]
        return jnp.concatenate([jnp.concatenate(real, axis=1), jnp.concatenate(imag, axis=1)], axis=0).astype(BF16)

    def multiply(left, right):
        return lax.dot_general(left, right, (((1,), (1,)), ((), ())), preferred_element_type=F32)

    def place(q, t, out):
        for a in range(OWN):
            acc[a, q, 6 * t : 6 * t + 8, :] += out[8 * a : 8 * a + 8]

    def squares(q, t, first, last):
        total = None
        for r in range(first, last):
            p, v = planes(othf, q, t, r)
            term = jnp.concatenate([p * p, v * v], axis=1)
            total = term if total is None else total + term
        return total

    acc[...] = jnp.zeros_like(acc)
    power[...] = jnp.zeros_like(power)
    pad = 2 * OWN * TILES
    ownf[:, :, pad:, :] = jnp.zeros((5, QUARTERS, 8, 128), F32)
    othf[:, :, pad:, :] = jnp.zeros((5, QUARTERS, 8, 128), F32)
    nothing = jnp.zeros((32, 256 * TOP), BF16)

    def own_quarter(q, carry):
        @pl.when(core == 0)
        def _():
            local_top(q).wait()
            to_core0(q).wait_recv()

        @pl.when(core == 1)
        def _():
            local_mid(q).wait()
            to_core1(q).wait_recv()

        lay(own, ownf, q, RIM, 5)
        for t in range(TILES):
            expand(q, t, RIM, 5)
        for t in range(TILES):
            right = jnp.concatenate([data(ownf, q, t, RIM, 5), nothing], axis=0)
            place(q, t, multiply(masked[q, t, :, 256 * RIM :], right))
        return carry

    lax.fori_loop(0, QUARTERS, own_quarter, 0)

    loads[2].wait()
    loads[3].wait()
    phi[...] = jnp.zeros_like(phi)
    for s in range(2):
        rows = screens[s]
        picked = jnp.where(core == 0, rows[:, 0, :], rows[:, 1, :])
        phi[16 * s : 16 * s + OWN, :] = picked
    trig[0] = jnp.cos(phi[...])
    trig[1] = jnp.sin(phi[...])

    tab_chip.wait_recv()

    @pl.when(both(core == 1, has_down))
    def _():
        for c in range(2):
            tab_up(c).wait_recv()

    slot = iota((16, 128), 0)
    own_index = jnp.where(slot < OWN, OWN * y + slot, -9)
    oth_index = jnp.where(slot < OWN, OWN * (y + 1) + slot, -9)
    partners[...] = jnp.full((16, 128), -1, I32)
    for b in range(2):
        partners[ACQ * b : ACQ * (b + 1), :] = othtab[b, 0:ACQ, :]
    other_table = partners[...]
    for a in range(OWN):
        k = a
        cos_a, sin_a = trig[0, k : k + 1, :], trig[1, k : k + 1, :]
        line = owntab[a // ACQ, a % ACQ : a % ACQ + 1, :]
        theirs = jnp.where(other_table == OWN * y + a, 1.0, 0.0)
        hits = (
            jnp.where(line == own_index, 1.0, 0.0),
            jnp.where(core == 0, jnp.where(line == oth_index, 1.0, 0.0), theirs),
        )
        for s in range(2):
            w = jnp.sum(hits[s], axis=1, keepdims=True)
            cos_b, sin_b = trig[0, 16 * s : 16 * s + 16, :], trig[1, 16 * s : 16 * s + 16, :]
            turn[s, a, 0] = w * (cos_a * cos_b + sin_a * sin_b)
            turn[s, a, 1] = w * (sin_a * cos_b - cos_a * sin_b)
            turn[s, a, 2] = jnp.broadcast_to(w, (16, 128))

    def other_quarter(q, carry):
        @pl.when(both(core == 0, has_up))
        def _():
            for b in range(2):
                wide(q, 0, 0, TOP, oth, RIM, me, oth_recv.at[q, b]).wait_recv()

        @pl.when(both(core == 1, has_down))
        def _():
            for b in range(2):
                wide(q, 1, TOP, MID, oth, 0, me, oth_recv.at[q, b]).wait_recv()

        lay(oth, othf, q, RIM, 5)
        for t in range(TILES):
            right = jnp.concatenate([nothing, data(othf, q, t, RIM, 5)], axis=0)
            place(q, t, multiply(masked[q, t, :, 256 * RIM :], right))
            square[q, t] = squares(q, t, RIM, 5)
        return carry

    lax.fori_loop(0, QUARTERS, other_quarter, 0)

    @pl.when(has_rim)
    def _():
        for b in range(2):
            rim_copy(0, b, own, me, az).wait_recv()

        @pl.when(has_up)
        def _():
            for b in range(2):
                rim_copy(1, b, oth, me, az).wait_recv()

    def split(v):
        high = v.astype(BF16)
        return [high, (v - high.astype(F32)).astype(BF16)]

    def rim_quarter(q, carry):
        lay(own, ownf, q, 0, RIM)
        lay(oth, othf, q, 0, RIM)
        for t in range(TILES):
            expand(q, t, 0, RIM)
        for t in range(TILES):
            right = jnp.concatenate([data(ownf, q, t, 0, RIM), data(othf, q, t, 0, RIM)], axis=0)
            place(q, t, multiply(masked[q, t, :, : 256 * RIM], right))
            total = jnp.concatenate(split(square[q, t] + squares(q, t, 0, RIM)), axis=0)
            ones = jnp.concatenate([masks[t], masks[t]], axis=1)
            power[q, 6 * t : 6 * t + 8, :] += multiply(ones, total)[0:8]
        return carry

    lax.fori_loop(0, QUARTERS, rim_quarter, 0)

    for a in range(OWN):
        turned[a] = jnp.transpose(acc[a].reshape(128, 64))
    summed = jnp.transpose(power[...].reshape(128, 32))
    othpow[...] = jnp.where(iota((16, 128), 0) < OWN, summed[0:16] + summed[16:32], 1.0)

    mypow[...] = jnp.ones_like(mypow)
    for a in range(OWN):
        mypow[a : a + 1, :] = turned[a, a : a + 1, :]

    first = jnp.where(core == 0, 1.0, 0.0).astype(F32)
    sums[...] = jnp.zeros_like(sums)
    gain = [jnp.zeros((16, 128), F32), jnp.zeros((16, 128), F32)]
    loss = jnp.zeros((16, 128), F32)
    for a in range(OWN):
        k = a
        slopes, misses = [], []
        for s, powers in enumerate((mypow[...], othpow[...])):
            real, imag = turned[a, 32 * s : 32 * s + 16, :], turned[a, 32 * s + 16 : 32 * s + 32, :]
            norm = lax.rsqrt(mypow[k : k + 1, :] * powers + EPSILON)
            cosine, sine = turn[s, a, 0], turn[s, a, 1]
            slope = norm * (imag * cosine - real * sine)
            gain[s] += slope
            slopes.append(slope)
            misses.append(turn[s, a, 2] - norm * (real * cosine + imag * sine))
        loss += misses[1]
        sums[0, k : k + 1, :] = -jnp.sum(slopes[0] + slopes[1], axis=0, keepdims=True)
        sums[1, k : k + 1, :] = jnp.sum(misses[0] + first * misses[1], axis=0, keepdims=True)
    sums[0] += gain[0]
    other_sums[0] = gain[1]
    other_sums[1] = (1.0 - first) * loss
    for b in range(2):
        for f in range(2):
            msg_own[b, 8 * f : 8 * f + ACQ, :] = sums[f, ACQ * b : ACQ * (b + 1), :]
            msg_oth[b, 8 * f : 8 * f + ACQ, :] = other_sums[f, ACQ * b : ACQ * (b + 1), :]
    fin_chip = small(2, msg_own.at[1 - core], fin_own.at[core], 2 * y + 1 - core, 3)
    fin_chip.start()

    def fin_side(b):
        return small(3 + b, msg_oth.at[b], fin_oth.at[core], 2 * side + b, 4 + core)

    @pl.when(has_side)
    def _():
        for b in range(2):
            fin_side(b).start()

    fin_own[core] = msg_own[core]
    fin_chip.wait_recv()

    @pl.when(has_down)
    def _():
        small(3, msg_oth.at[0], fin_oth.at[0], me, 4).wait_recv()

    @pl.when(has_up)
    def _():
        small(3, msg_oth.at[1], fin_oth.at[1], me, 5).wait_recv()

    for j in range(2):
        total = fin_own[j] + fin_oth[j]
        grad_ref[:, j, :] = total[0:ACQ]
        misfit_ref[:, j, :] = total[8 : 8 + ACQ]

    def drain(t, carry):
        @pl.when(has_down)
        def _():
            to_down(t).wait_send()

        @pl.when(has_up)
        def _():
            to_up(t).wait_send()

        @pl.when(core == 0)
        def _():
            to_core1(t).wait_send()

        @pl.when(core == 1)
        def _():
            to_core0(t).wait_send()

        return carry

    lax.fori_loop(0, QUARTERS, drain, 0)

    @pl.when(has_next)
    def _():
        rim_copy(0, core, own, 2 * y, az_next).wait_send()

        @pl.when(has_down)
        def _():
            rim_copy(1, core, oth, 2 * down, az_next).wait_send()

    tab_chip.wait_send()

    @pl.when(has_up)
    def _():
        tab_up(core).wait_send()

    fin_chip.wait_send()

    @pl.when(has_side)
    def _():
        for b in range(2):
            fin_side(b).wait_send()


def local(chips, slabs, complex_slabs, secondaries, pair_counts, phase_screens):
    columns = complex_slabs.shape[3]
    x = jnp.transpose(complex_slabs, (0, 2, 1, 3))
    vmem = pl.BlockSpec(memory_space=pltpu.VMEM)
    hbm = pl.BlockSpec(memory_space=pltpu.HBM)
    out = jax.ShapeDtypeStruct((ACQ, 2, 128), F32)
    return pl.pallas_call(
        functools.partial(kernel, chips, slabs),
        out_shape=(out, out),
        in_specs=[hbm] * 4,
        out_specs=(vmem, vmem),
        scratch_shapes=[
            pltpu.VMEM(secondaries.shape, I32),
            pltpu.SMEM(pair_counts.shape, I32),
            pltpu.VMEM((2, OWN, 2, 128), F32),
            pltpu.VMEM((2, ACQ, 5, 2, columns), BF16),
            pltpu.VMEM((2, ACQ, 5, 2, columns), BF16),
            pltpu.VMEM((5, QUARTERS, 2 * OWN * TILES + 8, 128), F32),
            pltpu.VMEM((5, QUARTERS, 2 * OWN * TILES + 8, 128), F32),
            pltpu.VMEM((QUARTERS, TILES, 8 * OWN, 256 * 5), BF16),
            pltpu.VMEM((OWN, QUARTERS, 32, 64), F32),
            pltpu.VMEM((OWN, 64, 128), F32),
            pltpu.VMEM((QUARTERS, TILES, 16, 256), F32),
            pltpu.VMEM((QUARTERS, 32, 32), F32),
            pltpu.VMEM((8, 128), I32),
            pltpu.VMEM((2, 8, 128), I32),
            pltpu.VMEM((2, 8, 128), I32),
            pltpu.VMEM((16, 128), I32),
            pltpu.VMEM((16, 128), F32),
            pltpu.VMEM((16, 128), F32),
            pltpu.VMEM((32, 128), F32),
            pltpu.VMEM((2, 32, 128), F32),
            pltpu.VMEM((2, OWN, 3, 16, 128), F32),
            pltpu.VMEM((2, 16, 128), F32),
            pltpu.VMEM((2, 16, 128), F32),
            pltpu.VMEM((2, 16, 128), F32),
            pltpu.VMEM((2, 16, 128), F32),
            pltpu.VMEM((2, 16, 128), F32),
            pltpu.VMEM((2, 16, 128), F32),
            pltpu.SemaphoreType.DMA((4,)),
            pltpu.SemaphoreType.DMA((QUARTERS,)),
            pltpu.SemaphoreType.DMA((QUARTERS, 3)),
            pltpu.SemaphoreType.DMA((2,)),
            pltpu.SemaphoreType.DMA((QUARTERS, 2)),
            pltpu.SemaphoreType.DMA((QUARTERS,)),
            pltpu.SemaphoreType.DMA((2, 2)),
            pltpu.SemaphoreType.DMA((5,)),
            pltpu.SemaphoreType.DMA((6,)),
        ],
        compiler_params=pltpu.CompilerParams(
            collective_id=0, has_side_effects=True, vmem_limit_bytes=56 * 1024 * 1024
        ),
    )(x, secondaries, pair_counts, phase_screens)


def solution(mesh):
    return jax.shard_map(
        functools.partial(local, mesh.shape["acq"] // 2, mesh.shape["az"]),
        mesh=mesh,
        in_specs=(P("acq", None, "az", None), P("acq", None), P("acq"), P(None, "az", None)),
        out_specs=(P("acq", "az", None), P("acq", "az", None)),
        check_vma=False,
    )
```

time: 30.4 us -> 27.6 us (0.908)
  Pallas kernels: 26.4 us -> 24.8 us
  local copies, waits for them, and re-layouts: 3.11 us -> 1.89 us
    pallas_call x1, Pallas kernels: 26.4 us -> 24.8 us  [local(): pl.pallas_call(functools.partial(kernel, chips, slabs), out_shape=(out, o...]
    unnamed x11 -> x4, local copies, waits for them, and re-layouts: 3.11 us -> 1.89 us
where the time goes in v1:
time: 27.6 us; the launch traced here: 27.4 us
  Pallas kernels  24.8 us (90%)
  local copies, waits for them, and re-layouts  1.89 us (7%)
  between operations  0.65 us (2%)
    pallas_call x1, Pallas kernels, local(): pl.pallas_call(functools.partial(kernel, chips, slabs), out_shape=(out, o...  24.8 us
    unnamed x4, local copies, waits for them, and re-layouts  1.89 us

profile of v1, /device:TPU:39, one launch (start us, length us, event | category | flops | bytes accessed | tf_op | source)
XLA Modules:
  0.0 27.4 jit_solution(4856142604815264844)
XLA Ops:
  0.6 24.8 %shard_map.59 = (f32[6,2,128]{2,1,0:T(2,128)}, f32[6,2,128]{2,1,0:T(2,128)}) custom-call(bf16[6,10,2,2560]{3,2,1,0:T(2,128)(2,1)} %bitcast.1, s32[6,10]{1,0:T(8,128)} %sec_hbm.1, s32[6]{0:T(128)} %cnt_hbm.1, f32[96,2,128]{2,1,0:T(2,128)} %screens_hbm.1), custom_call_target="tpu_custom_call" | custom-call | tf_op jit(solution)/shard_map/pallas_call | solution.py:486
  25.5 0.0 copy-start
  25.5 1.3 %copy.8 = f32[6,2,128]{2,1,0:T(2,128)} copy(f32[6,2,128]{2,1,0:T(2,128)} %get-tuple-element.4) | data formatting | bytes 12288
  26.8 0.0 copy-done
  26.8 0.6 %copy.9 = f32[6,2,128]{2,1,0:T(2,128)} copy(f32[6,2,128]{2,1,0:T(2,128)S(1)} %copy-done) | data formatting | bytes 12288
Async XLA Ops:
  25.5 1.3 %copy-start = (f32[6,2,128]{2,1,0:T(2,128)S(1)}, f32[6,2,128]{2,1,0:T(2,128)}, u32[]{:S(2)}) copy-start(f32[6,2,128]{2,1,0:T(2,128)} %get-tuple-element.5) | copy-start | bytes 18436

commit v2 on v1

--- a/solution.py
+++ b/solution.py
@@ -14,6 +14,7 @@
 ACQ = 6
 OWN = 12
 QUARTERS, TILES, QUARTER = 4, 5, 640
+RUN = 8
 TOP, MID, RIM = 3, 5, 2
 
 
@@ -27,7 +28,7 @@
     grad_ref, misfit_ref,
     secs, cnts, screens, own, oth, ownf, othf, masked, acc, turned, square, power,
     mytab, owntab, othtab, partners, mypow, othpow, phi, trig, turn, sums, other_sums, msg_own, msg_oth, fin_own, fin_oth,
-    load_sem, local_sem, send_sem, rim_send, oth_recv, own_recv, rim_recv, small_send, small_recv,
+    load_sem, local_sem, send_sem, rim_send, chip_send, oth_recv, own_recv, rim_recv, small_send, small_recv,
 ):
     me = lax.axis_index("acq")
     az = lax.axis_index("az")
@@ -53,25 +54,16 @@
     def columns(q):
         return pl.ds(pl.multiple_of(QUARTER * q, 128), QUARTER)
 
-    def local_top(q):
-        return pltpu.make_async_copy(
-            x_hbm.at[:, pl.ds(0, TOP), :, columns(q)], own.at[0, :, pl.ds(RIM, TOP), :, columns(q)], local_sem.at[q]
-        )
-
-    def local_mid(q):
-        return pltpu.make_async_copy(
-            x_hbm.at[:, pl.ds(TOP, MID), :, columns(q)], own.at[1, :, :, :, columns(q)], local_sem.at[q]
-        )
+    local_top = pltpu.make_async_copy(x_hbm.at[:, pl.ds(0, TOP)], own.at[0, :, pl.ds(RIM, TOP)], local_sem)
+    local_mid = pltpu.make_async_copy(x_hbm.at[:, pl.ds(TOP, MID)], own.at[1], local_sem)
 
     @pl.when(core == 0)
     def _():
-        for q in range(QUARTERS):
-            local_top(q).start()
+        local_top.start()
 
     @pl.when(core == 1)
     def _():
-        for q in range(QUARTERS):
-            local_mid(q).start()
+        local_mid.start()
 
     fin_oth[...] = jnp.zeros_like(fin_oth)
     msg_own[...] = jnp.zeros_like(msg_own)
@@ -118,6 +110,81 @@
     @pl.when(jnp.logical_not(has_side))
     def _():
         oth[...] = jnp.zeros_like(oth)
+
+    def small(k, src, dst, a, sem):
+        return pltpu.make_async_remote_copy(
+            src_ref=src, dst_ref=dst, send_sem=small_send.at[k], recv_sem=small_recv.at[sem],
+            device_id=(a, az), device_id_type=MESH,
+        )
+
+    def wide(q, k, first, rows, buffer, start, a, sem):
+        return pltpu.make_async_remote_copy(
+            src_ref=x_hbm.at[:, pl.ds(first, rows), :, columns(q)],
+            dst_ref=buffer.at[core, :, pl.ds(start, rows), :, columns(q)],
+            send_sem=send_sem.at[q, k], recv_sem=sem,
+            device_id=(a, az), device_id_type=MESH,
+        )
+
+    def to_down(q):
+        return wide(q, 0, 0, TOP, oth, RIM, 2 * down, oth_recv.at[q, core])
+
+    def to_up(q):
+        return wide(q, 1, TOP, MID, oth, 0, 2 * up + 1, oth_recv.at[q, core])
+
+    def chip_copy(first, rows, start, a):
+        return pltpu.make_async_remote_copy(
+            src_ref=x_hbm.at[:, pl.ds(first, rows)], dst_ref=own.at[core, :, pl.ds(start, rows)],
+            send_sem=chip_send, recv_sem=own_recv, device_id=(a, az), device_id_type=MESH,
+        )
+
+    to_core1 = chip_copy(TOP, MID, 0, 2 * y + 1)
+    to_core0 = chip_copy(0, TOP, RIM, 2 * y)
+
+    def rim_copy(k, block, buffer, a, z):
+        return pltpu.make_async_remote_copy(
+            src_ref=x_hbm.at[:, pl.ds(TOP + MID, RIM)],
+            dst_ref=buffer.at[block, :, pl.ds(0, RIM)],
+            send_sem=rim_send.at[k], recv_sem=rim_recv.at[k, block],
+            device_id=(a, z), device_id_type=MESH,
+        )
+
+    pl.semaphore_wait(barrier, expected)
+
+    @pl.when(has_next)
+    def _():
+        rim_copy(0, core, own, 2 * y, az_next).start()
+
+        @pl.when(has_down)
+        def _():
+            rim_copy(1, core, oth, 2 * down, az_next).start()
+
+    @pl.when(core == 0)
+    def _():
+        to_core1.start()
+
+    @pl.when(core == 1)
+    def _():
+        to_core0.start()
+
+    @pl.when(has_up)
+    def _():
+        for q in range(QUARTERS):
+            to_up(q).start()
+
+    rim_first = both(has_next, az % RUN == RUN - 1)
+
+    @pl.when(rim_first)
+    def _():
+        rim_copy(0, core, own, 2 * y, az_next).wait_send()
+
+        @pl.when(has_down)
+        def _():
+            rim_copy(1, core, oth, 2 * down, az_next).wait_send()
+
+    @pl.when(has_down)
+    def _():
+        for q in range(QUARTERS):
+            to_down(q).start()
 
     loads[0].wait()
     loads[1].wait()
@@ -129,71 +196,6 @@
     mytab[...] = jnp.where(iota((8, 128), 1) < slots, mytab[...], -1)
     owntab[core] = mytab[...]
 
-    def small(k, src, dst, a, sem):
-        return pltpu.make_async_remote_copy(
-            src_ref=src, dst_ref=dst, send_sem=small_send.at[k], recv_sem=small_recv.at[sem],
-            device_id=(a, az), device_id_type=MESH,
-        )
-
-    def wide(q, k, first, rows, buffer, start, a, sem):
-        return pltpu.make_async_remote_copy(
-            src_ref=x_hbm.at[:, pl.ds(first, rows), :, columns(q)],
-            dst_ref=buffer.at[core, :, pl.ds(start, rows), :, columns(q)],
-            send_sem=send_sem.at[q, k], recv_sem=sem,
-            device_id=(a, az), device_id_type=MESH,
-        )
-
-    def to_down(q):
-        return wide(q, 0, 0, TOP, oth, RIM, 2 * down, oth_recv.at[q, core])
-
-    def to_up(q):
-        return wide(q, 1, TOP, MID, oth, 0, 2 * up + 1, oth_recv.at[q, core])
-
-    def to_core1(q):
-        return wide(q, 2, TOP, MID, own, 0, 2 * y + 1, own_recv.at[q])
-
-    def to_core0(q):
-        return wide(q, 2, 0, TOP, own, RIM, 2 * y, own_recv.at[q])
-
-    def rim_copy(k, block, buffer, a, z):
-        return pltpu.make_async_remote_copy(
-            src_ref=x_hbm.at[:, pl.ds(TOP + MID, RIM)],
-            dst_ref=buffer.at[block, :, pl.ds(0, RIM)],
-            send_sem=rim_send.at[k], recv_sem=rim_recv.at[k, block],
-            device_id=(a, z), device_id_type=MESH,
-        )
-
-    pl.semaphore_wait(barrier, expected)
-
-    @pl.when(has_next)
-    def _():
-        rim_copy(0, core, own, 2 * y, az_next).start()
-
-        @pl.when(has_down)
-        def _():
-            rim_copy(1, core, oth, 2 * down, az_next).start()
-
-    def start_wide(q, carry):
-        @pl.when(core == 0)
-        def _():
-            to_core1(q).start()
-
-        @pl.when(core == 1)
-        def _():
-            to_core0(q).start()
-
-        @pl.when(has_down)
-        def _():
-            to_down(q).start()
-
-        @pl.when(has_up)
-        def _():
-            to_up(q).start()
-
-        return carry
-
-    lax.fori_loop(0, QUARTERS, start_wide, 0)
-
     tab_chip = small(0, mytab, owntab.at[core], 2 * y + 1 - core, 0)
     tab_chip.start()
 
@@ -219,15 +221,15 @@
     masks = [cell_mask(t) for t in range(TILES)]
 
     def expand(q, t, first, last):
+        parts = []
         for r in range(first, last):
             for c in range(2):
-                start = 256 * r + 128 * c
-                for a in range(0, OWN, 2):
+                lines = []
+                for a in range(OWN):
                     source = 2 * OWN * t + OWN * c + a
-                    low = jnp.broadcast_to(ownf[r, q, source : source + 1, :], (8, 128))
-                    high = jnp.broadcast_to(ownf[r, q, source + 1 : source + 2, :], (8, 128))
-                    block = jnp.concatenate([low, high], axis=0).astype(BF16) * masks[t]
-                    masked[q, t, 8 * a : 8 * a + 16, start : start + 128] = block
+                    lines.append(jnp.broadcast_to(ownf[r, q, source : source + 1, :], (8, 128)))
+                parts.append(jnp.concatenate(lines, axis=0).astype(BF16) * jnp.concatenate([masks[t]] * (OWN // 2), axis=0))
+        return jnp.concatenate(parts, axis=1)
 
     def planes(rows, q, t, r):
         start = 2 * OWN * t
@@ -244,9 +246,12 @@
     def multiply(left, right):
         return lax.dot_general(left, right, (((1,), (1,)), ((), ())), preferred_element_type=F32)
 
-    def place(q, t, out):
-        for a in range(OWN):
-            acc[a, q, 6 * t : 6 * t + 8, :] += out[8 * a : 8 * a + 8]
+    even = iota((8, 128), 1) < 64
+
+    def place(q, t, left, right):
+        out = multiply(left, jnp.concatenate([right, right], axis=0))
+        for p in range(OWN // 2):
+            acc[p, q, 6 * t : 6 * t + 8, :] += jnp.where(even, out[16 * p : 16 * p + 8], out[16 * p + 8 : 16 * p + 16])
 
     def squares(q, t, first, last):
         total = None
@@ -258,28 +263,28 @@
 
     acc[...] = jnp.zeros_like(acc)
     power[...] = jnp.zeros_like(power)
+    square[...] = jnp.zeros_like(square)
     pad = 2 * OWN * TILES
     ownf[:, :, pad:, :] = jnp.zeros((5, QUARTERS, 8, 128), F32)
     othf[:, :, pad:, :] = jnp.zeros((5, QUARTERS, 8, 128), F32)
     nothing = jnp.zeros((32, 256 * TOP), BF16)
 
+    @pl.when(core == 0)
+    def _():
+        local_top.wait()
+        to_core0.wait_recv()
+
+    @pl.when(core == 1)
+    def _():
+        local_mid.wait()
+        to_core1.wait_recv()
+
     def own_quarter(q, carry):
-        @pl.when(core == 0)
-        def _():
-            local_top(q).wait()
-            to_core0(q).wait_recv()
-
-        @pl.when(core == 1)
-        def _():
-            local_mid(q).wait()
-            to_core1(q).wait_recv()
-
         lay(own, ownf, q, RIM, 5)
         for t in range(TILES):
-            expand(q, t, RIM, 5)
-        for t in range(TILES):
-            right = jnp.concatenate([data(ownf, q, t, RIM, 5), nothing], axis=0)
-            place(q, t, multiply(masked[q, t, :, 256 * RIM :], right))
+            left = expand(q, t, RIM, 5)
+            masked[q, t] = left
+            place(q, t, left, jnp.concatenate([data(ownf, q, t, RIM, 5), nothing], axis=0))
         return carry
 
     lax.fori_loop(0, QUARTERS, own_quarter, 0)
@@ -324,6 +329,36 @@
             turn[s, a, 1] = w * (sin_a * cos_b - cos_a * sin_b)
             turn[s, a, 2] = jnp.broadcast_to(w, (16, 128))
 
+    def rim_phase():
+        @pl.when(has_rim)
+        def _():
+            for b in range(2):
+                rim_copy(0, b, own, me, az).wait_recv()
+
+            @pl.when(has_up)
+            def _():
+                for b in range(2):
+                    rim_copy(1, b, oth, me, az).wait_recv()
+
+        def rim_half(h, carry):
+            for q in (2 * h, 2 * h + 1):
+                lay(own, ownf, q, 0, RIM)
+                lay(oth, othf, q, 0, RIM)
+            for q in (2 * h, 2 * h + 1):
+                for t in range(TILES):
+                    right = jnp.concatenate([data(ownf, q, t, 0, RIM), data(othf, q, t, 0, RIM)], axis=0)
+                    place(q, t, expand(q, t, 0, RIM), right)
+                    square[q, t] += squares(q, t, 0, RIM)
+            return carry
+
+        lax.fori_loop(0, QUARTERS // 2, rim_half, 0)
+
+    rim_last = jnp.logical_or(core == 1, az % RUN == 0)
+
+    @pl.when(jnp.logical_not(rim_last))
+    def _():
+        rim_phase()
+
     def other_quarter(q, carry):
         @pl.when(both(core == 0, has_up))
         def _():
@@ -338,43 +373,27 @@
         lay(oth, othf, q, RIM, 5)
         for t in range(TILES):
             right = jnp.concatenate([nothing, data(othf, q, t, RIM, 5)], axis=0)
-            place(q, t, multiply(masked[q, t, :, 256 * RIM :], right))
-            square[q, t] = squares(q, t, RIM, 5)
+            place(q, t, masked[q, t], right)
+            square[q, t] += squares(q, t, RIM, 5)
         return carry
 
     lax.fori_loop(0, QUARTERS, other_quarter, 0)
 
-    @pl.when(has_rim)
-    def _():
-        for b in range(2):
-            rim_copy(0, b, own, me, az).wait_recv()
-
-        @pl.when(has_up)
-        def _():
-            for b in range(2):
-                rim_copy(1, b, oth, me, az).wait_recv()
+    @pl.when(rim_last)
+    def _():
+        rim_phase()
 
     def split(v):
         high = v.astype(BF16)
         return [high, (v - high.astype(F32)).astype(BF16)]
 
-    def rim_quarter(q, carry):
-        lay(own, ownf, q, 0, RIM)
-        lay(oth, othf, q, 0, RIM)
+    for q in range(QUARTERS):
         for t in range(TILES):
-            expand(q, t, 0, RIM)
-        for t in range(TILES):
-            right = jnp.concatenate([data(ownf, q, t, 0, RIM), data(othf, q, t, 0, RIM)], axis=0)
-            place(q, t, multiply(masked[q, t, :, : 256 * RIM], right))
-            total = jnp.concatenate(split(square[q, t] + squares(q, t, 0, RIM)), axis=0)
             ones = jnp.concatenate([masks[t], masks[t]], axis=1)
-            power[q, 6 * t : 6 * t + 8, :] += multiply(ones, total)[0:8]
-        return carry
-
-    lax.fori_loop(0, QUARTERS, rim_quarter, 0)
-
-    for a in range(OWN):
-        turned[a] = jnp.transpose(acc[a].reshape(128, 64))
+            power[q, 6 * t : 6 * t + 8, :] += multiply(ones, jnp.concatenate(split(square[q, t]), axis=0))[0:8]
+
+    for p in range(OWN // 2):
+        turned[2 * p : 2 * p + 2] = jnp.transpose(acc[p].reshape(128, 128)).reshape(2, 64, 128)
     summed = jnp.transpose(power[...].reshape(128, 32))
     othpow[...] = jnp.where(iota((16, 128), 0) < OWN, summed[0:16] + summed[16:32], 1.0)
 
@@ -419,6 +438,43 @@
             fin_side(b).start()
 
     fin_own[core] = msg_own[core]
+
+    @pl.when(has_down)
+    def _():
+        for q in range(QUARTERS):
+            to_down(q).wait_send()
+
+    @pl.when(has_up)
+    def _():
+        for q in range(QUARTERS):
+            to_up(q).wait_send()
+
+        tab_up(core).wait_send()
+
+    @pl.when(core == 0)
+    def _():
+        to_core1.wait_send()
+
+    @pl.when(core == 1)
+    def _():
+        to_core0.wait_send()
+
+    @pl.when(both(has_next, jnp.logical_not(rim_first)))
+    def _():
+        rim_copy(0, core, own, 2 * y, az_next).wait_send()
+
+        @pl.when(has_down)
+        def _():
+            rim_copy(1, core, oth, 2 * down, az_next).wait_send()
+
+    tab_chip.wait_send()
+    fin_chip.wait_send()
+
+    @pl.when(has_side)
+    def _():
+        for b in range(2):
+            fin_side(b).wait_send()
+
     fin_chip.wait_recv()
 
     @pl.when(has_down)
@@ -433,48 +489,6 @@
         total = fin_own[j] + fin_oth[j]
         grad_ref[:, j, :] = total[0:ACQ]
         misfit_ref[:, j, :] = total[8 : 8 + ACQ]
-
-    def drain(t, carry):
-        @pl.when(has_down)
-        def _():
-            to_down(t).wait_send()
-
-        @pl.when(has_up)
-        def _():
-            to_up(t).wait_send()
-
-        @pl.when(core == 0)
-        def _():
-            to_core1(t).wait_send()
-
-        @pl.when(core == 1)
-        def _():
-            to_core0(t).wait_send()
-
-        return carry
-
-    lax.fori_loop(0, QUARTERS, drain, 0)
-
-    @pl.when(has_next)
-    def _():
-        rim_copy(0, core, own, 2 * y, az_next).wait_send()
-
-        @pl.when(has_down)
-        def _():
-            rim_copy(1, core, oth, 2 * down, az_next).wait_send()
-
-    tab_chip.wait_send()
-
-    @pl.when(has_up)
-    def _():
-        tab_up(core).wait_send()
-
-    fin_chip.wait_send()
-
-    @pl.when(has_side)
-    def _():
-        for b in range(2):
-            fin_side(b).wait_send()
 
 
 def local(chips, slabs, complex_slabs, secondaries, pair_counts, phase_screens):
@@ -496,8 +510,8 @@
             pltpu.VMEM((2, ACQ, 5, 2, columns), BF16),
             pltpu.VMEM((5, QUARTERS, 2 * OWN * TILES + 8, 128), F32),
             pltpu.VMEM((5, QUARTERS, 2 * OWN * TILES + 8, 128), F32),
-            pltpu.VMEM((QUARTERS, TILES, 8 * OWN, 256 * 5), BF16),
-            pltpu.VMEM((OWN, QUARTERS, 32, 64), F32),
+            pltpu.VMEM((QUARTERS, TILES, 8 * OWN, 256 * TOP), BF16),
+            pltpu.VMEM((OWN // 2, QUARTERS, 32, 128), F32),
             pltpu.VMEM((OWN, 64, 128), F32),
             pltpu.VMEM((QUARTERS, TILES, 16, 256), F32),
             pltpu.VMEM((QUARTERS, 32, 32), F32),
@@ -517,11 +531,12 @@
             pltpu.VMEM((2, 16, 128), F32),
             pltpu.VMEM((2, 16, 128), F32),
             pltpu.SemaphoreType.DMA((4,)),
-            pltpu.SemaphoreType.DMA((QUARTERS,)),
-            pltpu.SemaphoreType.DMA((QUARTERS, 3)),
+            pltpu.SemaphoreType.DMA,
+            pltpu.SemaphoreType.DMA((QUARTERS, 2)),
             pltpu.SemaphoreType.DMA((2,)),
+            pltpu.SemaphoreType.DMA,
             pltpu.SemaphoreType.DMA((QUARTERS, 2)),
-            pltpu.SemaphoreType.DMA((QUARTERS,)),
+            pltpu.SemaphoreType.DMA,
             pltpu.SemaphoreType.DMA((2, 2)),
             pltpu.SemaphoreType.DMA((5,)),
             pltpu.SemaphoreType.DMA((6,)),

time: 27.6 us -> 27 us (0.978)
  Pallas kernels: 24.8 us -> 24.3 us
    pallas_call x1, Pallas kernels: 24.8 us -> 24.3 us  [local(): pl.pallas_call(functools.partial(kernel, chips, slabs), out_shape=(out, o...]
where the time goes in v2:
time: 27 us; the launch traced here: 26.8 us
  Pallas kernels  24.3 us (90%)
  local copies, waits for them, and re-layouts  1.89 us (7%)
  between operations  0.65 us (2%)
    pallas_call x1, Pallas kernels, local(): pl.pallas_call(functools.partial(kernel, chips, slabs), out_shape=(out, o...  24.3 us
    unnamed x4, local copies, waits for them, and re-layouts  1.89 us

profile of v2, /device:TPU:39, one launch (start us, length us, event | category | flops | bytes accessed | tf_op | source)
XLA Modules:
  0.0 26.8 jit_solution(4193089876434559507)
XLA Ops:
  0.6 24.3 %shard_map.59 = (f32[6,2,128]{2,1,0:T(2,128)}, f32[6,2,128]{2,1,0:T(2,128)}) custom-call(bf16[6,10,2,2560]{3,2,1,0:T(2,128)(2,1)} %bitcast.1, s32[6,10]{1,0:T(8,128)} %sec_hbm.1, s32[6]{0:T(128)} %cnt_hbm.1, f32[96,2,128]{2,1,0:T(2,128)} %screens_hbm.1), custom_call_target="tpu_custom_call" | custom-call | tf_op jit(solution)/shard_map/pallas_call | solution.py:500
  24.9 0.0 copy-start
  24.9 1.3 %copy.8 = f32[6,2,128]{2,1,0:T(2,128)} copy(f32[6,2,128]{2,1,0:T(2,128)} %get-tuple-element.4) | data formatting | bytes 12288
  26.2 0.0 copy-done
  26.2 0.6 %copy.9 = f32[6,2,128]{2,1,0:T(2,128)} copy(f32[6,2,128]{2,1,0:T(2,128)S(1)} %copy-done) | data formatting | bytes 12288
Async XLA Ops:
  24.9 1.3 %copy-start = (f32[6,2,128]{2,1,0:T(2,128)S(1)}, f32[6,2,128]{2,1,0:T(2,128)}, u32[]{:S(2)}) copy-start(f32[6,2,128]{2,1,0:T(2,128)} %get-tuple-element.5) | copy-start | bytes 18436

commit v3 on v2

--- a/solution.py
+++ b/solution.py
@@ -25,8 +25,8 @@
 def kernel(
     chips, slabs,
     x_hbm, sec_hbm, cnt_hbm, screens_hbm,
-    grad_ref, misfit_ref,
-    secs, cnts, screens, own, oth, ownf, othf, masked, acc, turned, square, power,
+    out_ref,
+    secs, cnts, screens, own, oth, ownf, othf, masked, acc, turned, power,
     mytab, owntab, othtab, partners, mypow, othpow, phi, trig, turn, sums, other_sums, msg_own, msg_oth, fin_own, fin_oth,
     load_sem, local_sem, send_sem, rim_send, chip_send, oth_recv, own_recv, rim_recv, small_send, small_recv,
 ):
@@ -102,11 +102,6 @@
 
     expected = 1 + 2 * flag(has_up) + 2 * flag(has_down) + flag(has_next) + flag(both(has_next, has_down))
 
-    @pl.when(both(core == 0, jnp.logical_not(has_prev)))
-    def _():
-        own[:, :, 0:RIM] = jnp.zeros((2, ACQ, RIM, 2, QUARTERS * QUARTER), BF16)
-        oth[:, :, 0:RIM] = jnp.zeros((2, ACQ, RIM, 2, QUARTERS * QUARTER), BF16)
-
     @pl.when(jnp.logical_not(has_side))
     def _():
         oth[...] = jnp.zeros_like(oth)
@@ -140,23 +135,41 @@
     to_core1 = chip_copy(TOP, MID, 0, 2 * y + 1)
     to_core0 = chip_copy(0, TOP, RIM, 2 * y)
 
-    def rim_copy(k, block, buffer, a, z):
+    def rim_copy(k, q, block, buffer, a, z):
         return pltpu.make_async_remote_copy(
-            src_ref=x_hbm.at[:, pl.ds(TOP + MID, RIM)],
-            dst_ref=buffer.at[block, :, pl.ds(0, RIM)],
-            send_sem=rim_send.at[k], recv_sem=rim_recv.at[k, block],
+            src_ref=x_hbm.at[:, pl.ds(TOP + MID, RIM), :, columns(q)],
+            dst_ref=buffer.at[block, :, pl.ds(0, RIM), :, columns(q)],
+            send_sem=rim_send.at[k, q], recv_sem=rim_recv.at[k, block, q],
             device_id=(a, z), device_id_type=MESH,
         )
 
+    def own_rim(q):
+        return rim_copy(0, q, core, own, 2 * y, az_next)
+
+    def oth_rim(q):
+        return rim_copy(1, q, core, oth, 2 * down, az_next)
+
+    def wait_rims():
+        for q in range(QUARTERS):
+            own_rim(q).wait_send()
+
+        @pl.when(has_down)
+        def _():
+            for q in range(QUARTERS):
+                oth_rim(q).wait_send()
+
     pl.semaphore_wait(barrier, expected)
 
-    @pl.when(has_next)
-    def _():
-        rim_copy(0, core, own, 2 * y, az_next).start()
-
-        @pl.when(has_down)
-        def _():
-            rim_copy(1, core, oth, 2 * down, az_next).start()
+    @pl.when(both(has_next, has_down))
+    def _():
+        for q in range(QUARTERS):
+            own_rim(q).start()
+            oth_rim(q).start()
+
+    @pl.when(both(has_next, jnp.logical_not(has_down)))
+    def _():
+        for q in range(QUARTERS):
+            own_rim(q).start()
 
     @pl.when(core == 0)
     def _():
@@ -175,11 +188,7 @@
 
     @pl.when(rim_first)
     def _():
-        rim_copy(0, core, own, 2 * y, az_next).wait_send()
-
-        @pl.when(has_down)
-        def _():
-            rim_copy(1, core, oth, 2 * down, az_next).wait_send()
+        wait_rims()
 
     @pl.when(has_down)
     def _():
@@ -253,17 +262,21 @@
         for p in range(OWN // 2):
             acc[p, q, 6 * t : 6 * t + 8, :] += jnp.where(even, out[16 * p : 16 * p + 8], out[16 * p + 8 : 16 * p + 16])
 
-    def squares(q, t, first, last):
+    def split(v):
+        high = v.astype(BF16)
+        return [high, (v - high.astype(F32)).astype(BF16)]
+
+    def add_power(q, t, first, last):
         total = None
         for r in range(first, last):
             p, v = planes(othf, q, t, r)
             term = jnp.concatenate([p * p, v * v], axis=1)
             total = term if total is None else total + term
-        return total
+        ones = jnp.concatenate([masks[t], masks[t]], axis=1)
+        power[q, 6 * t : 6 * t + 8, :] += multiply(ones, jnp.concatenate(split(total), axis=0))[0:8]
 
     acc[...] = jnp.zeros_like(acc)
     power[...] = jnp.zeros_like(power)
-    square[...] = jnp.zeros_like(square)
     pad = 2 * OWN * TILES
     ownf[:, :, pad:, :] = jnp.zeros((5, QUARTERS, 8, 128), F32)
     othf[:, :, pad:, :] = jnp.zeros((5, QUARTERS, 8, 128), F32)
@@ -329,37 +342,25 @@
             turn[s, a, 1] = w * (sin_a * cos_b - cos_a * sin_b)
             turn[s, a, 2] = jnp.broadcast_to(w, (16, 128))
 
-    def rim_phase():
-        @pl.when(has_rim)
+    def rim_part(q):
+        @pl.when(core == 0)
         def _():
             for b in range(2):
-                rim_copy(0, b, own, me, az).wait_recv()
-
-            @pl.when(has_up)
-            def _():
-                for b in range(2):
-                    rim_copy(1, b, oth, me, az).wait_recv()
-
-        def rim_half(h, carry):
-            for q in (2 * h, 2 * h + 1):
-                lay(own, ownf, q, 0, RIM)
-                lay(oth, othf, q, 0, RIM)
-            for q in (2 * h, 2 * h + 1):
-                for t in range(TILES):
-                    right = jnp.concatenate([data(ownf, q, t, 0, RIM), data(othf, q, t, 0, RIM)], axis=0)
-                    place(q, t, expand(q, t, 0, RIM), right)
-                    square[q, t] += squares(q, t, 0, RIM)
-            return carry
-
-        lax.fori_loop(0, QUARTERS // 2, rim_half, 0)
-
-    rim_last = jnp.logical_or(core == 1, az % RUN == 0)
-
-    @pl.when(jnp.logical_not(rim_last))
-    def _():
-        rim_phase()
-
-    def other_quarter(q, carry):
+                rim_copy(0, q, b, own, me, az).wait_recv()
+
+        @pl.when(both(core == 0, has_up))
+        def _():
+            for b in range(2):
+                rim_copy(1, q, b, oth, me, az).wait_recv()
+
+        lay(own, ownf, q, 0, RIM)
+        lay(oth, othf, q, 0, RIM)
+        for t in range(TILES):
+            right = jnp.concatenate([data(ownf, q, t, 0, RIM), data(othf, q, t, 0, RIM)], axis=0)
+            place(q, t, expand(q, t, 0, RIM), right)
+            add_power(q, t, 0, RIM)
+
+    def main_part(q):
         @pl.when(both(core == 0, has_up))
         def _():
             for b in range(2):
@@ -374,23 +375,27 @@
         for t in range(TILES):
             right = jnp.concatenate([nothing, data(othf, q, t, RIM, 5)], axis=0)
             place(q, t, masked[q, t], right)
-            square[q, t] += squares(q, t, RIM, 5)
+            add_power(q, t, RIM, 5)
+
+    rim_late = az % RUN == 0
+    has_first = jnp.logical_or(core == 1, has_prev)
+
+    def step(i, carry):
+        half = i // QUARTERS
+        rim = jnp.where(core == 1, i % 2, jnp.where(rim_late, half, 1 - half))
+        q = jnp.where(core == 1, i // 2, i % QUARTERS)
+
+        @pl.when(both(rim == 1, has_first))
+        def _():
+            rim_part(q)
+
+        @pl.when(rim == 0)
+        def _():
+            main_part(q)
+
         return carry
 
-    lax.fori_loop(0, QUARTERS, other_quarter, 0)
-
-    @pl.when(rim_last)
-    def _():
-        rim_phase()
-
-    def split(v):
-        high = v.astype(BF16)
-        return [high, (v - high.astype(F32)).astype(BF16)]
-
-    for q in range(QUARTERS):
-        for t in range(TILES):
-            ones = jnp.concatenate([masks[t], masks[t]], axis=1)
-            power[q, 6 * t : 6 * t + 8, :] += multiply(ones, jnp.concatenate(split(square[q, t]), axis=0))[0:8]
+    lax.fori_loop(0, 2 * QUARTERS, step, 0)
 
     for p in range(OWN // 2):
         turned[2 * p : 2 * p + 2] = jnp.transpose(acc[p].reshape(128, 128)).reshape(2, 64, 128)
@@ -461,11 +466,7 @@
 
     @pl.when(both(has_next, jnp.logical_not(rim_first)))
     def _():
-        rim_copy(0, core, own, 2 * y, az_next).wait_send()
-
-        @pl.when(has_down)
-        def _():
-            rim_copy(1, core, oth, 2 * down, az_next).wait_send()
+        wait_rims()
 
     tab_chip.wait_send()
     fin_chip.wait_send()
@@ -487,8 +488,8 @@
 
     for j in range(2):
         total = fin_own[j] + fin_oth[j]
-        grad_ref[:, j, :] = total[0:ACQ]
-        misfit_ref[:, j, :] = total[8 : 8 + ACQ]
+        out_ref[0, :, j, :] = total[0:ACQ]
+        out_ref[1, :, j, :] = total[8 : 8 + ACQ]
 
 
 def local(chips, slabs, complex_slabs, secondaries, pair_counts, phase_screens):
@@ -496,12 +497,12 @@
     x = jnp.transpose(complex_slabs, (0, 2, 1, 3))
     vmem = pl.BlockSpec(memory_space=pltpu.VMEM)
     hbm = pl.BlockSpec(memory_space=pltpu.HBM)
-    out = jax.ShapeDtypeStruct((ACQ, 2, 128), F32)
-    return pl.pallas_call(
+    out = jax.ShapeDtypeStruct((2, ACQ, 2, 128), F32)
+    both = pl.pallas_call(
         functools.partial(kernel, chips, slabs),
-        out_shape=(out, out),
+        out_shape=out,
         in_specs=[hbm] * 4,
-        out_specs=(vmem, vmem),
+        out_specs=vmem,
         scratch_shapes=[
             pltpu.VMEM(secondaries.shape, I32),
             pltpu.SMEM(pair_counts.shape, I32),
@@ -513,7 +514,6 @@
             pltpu.VMEM((QUARTERS, TILES, 8 * OWN, 256 * TOP), BF16),
             pltpu.VMEM((OWN // 2, QUARTERS, 32, 128), F32),
             pltpu.VMEM((OWN, 64, 128), F32),
-            pltpu.VMEM((QUARTERS, TILES, 16, 256), F32),
             pltpu.VMEM((QUARTERS, 32, 32), F32),
             pltpu.VMEM((8, 128), I32),
             pltpu.VMEM((2, 8, 128), I32),
@@ -533,11 +533,11 @@
             pltpu.SemaphoreType.DMA((4,)),
             pltpu.SemaphoreType.DMA,
             pltpu.SemaphoreType.DMA((QUARTERS, 2)),
-            pltpu.SemaphoreType.DMA((2,)),
+            pltpu.SemaphoreType.DMA((2, QUARTERS)),
             pltpu.SemaphoreType.DMA,
             pltpu.SemaphoreType.DMA((QUARTERS, 2)),
             pltpu.SemaphoreType.DMA,
-            pltpu.SemaphoreType.DMA((2, 2)),
+            pltpu.SemaphoreType.DMA((2, 2, QUARTERS)),
             pltpu.SemaphoreType.DMA((5,)),
             pltpu.SemaphoreType.DMA((6,)),
         ],
@@ -545,6 +545,7 @@
             collective_id=0, has_side_effects=True, vmem_limit_bytes=56 * 1024 * 1024
         ),
     )(x, secondaries, pair_counts, phase_screens)
+    return both[0], both[1]
 
 
 def solution(mesh):

time: 27 us -> 25.6 us (0.948)
  Pallas kernels: 24.3 us -> 23.5 us
  local copies, waits for them, and re-layouts: 1.89 us -> 1.31 us
    unnamed x4 -> x0, local copies, waits for them, and re-layouts: 1.89 us -> none
    squeeze x0 -> x1, local copies, waits for them, and re-layouts: none -> 1.31 us  [local(): return (both[0], both[1])]
    pallas_call x1, Pallas kernels: 24.3 us -> 23.5 us  [local(): pl.pallas_call(functools.partial(kernel, chips, slabs), out_shape=out, in...]
where the time goes in v3:
time: 25.6 us; the launch traced here: 25.5 us
  Pallas kernels  23.5 us (92%)
  local copies, waits for them, and re-layouts  1.31 us (5%)
  between operations  0.64 us (2%)
    pallas_call x1, Pallas kernels, local(): pl.pallas_call(functools.partial(kernel, chips, slabs), out_shape=out, in...  23.5 us
    squeeze x1, local copies, waits for them, and re-layouts, local(): return (both[0], both[1])  1.31 us

profile of v3, /device:TPU:39, one launch (start us, length us, event | category | flops | bytes accessed | tf_op | source)
XLA Modules:
  0.0 25.5 jit_solution(3541361184644533853)
XLA Ops:
  0.6 23.5 %shard_map.59 = f32[2,6,2,128]{3,2,1,0:T(2,128)} custom-call(bf16[6,10,2,2560]{3,2,1,0:T(2,128)(2,1)} %bitcast.5, s32[6,10]{1,0:T(8,128)} %sec_hbm.1, s32[6]{0:T(128)} %cnt_hbm.1, f32[96,2,128]{2,1,0:T(2,128)} %screens_hbm.1), custom_call_target="tpu_custom_call" | custom-call | tf_op jit(solution)/shard_map/pallas_call | solution.py:501
  24.1 1.3 %slice_bitcast_fusion = (f32[6,2,128]{2,1,0:T(2,128)}, f32[6,2,128]{2,1,0:T(2,128)}) fusion(f32[2,6,2,128]{3,2,1,0:T(2,128)} %shard_map.59), kind=kLoop, calls=%fused_computation | loop fusion | bytes 24576 | tf_op jit(solution)/shard_map/squeeze | solution.py:548

commit v4 on v3

--- a/solution.py
+++ b/solution.py
@@ -14,6 +14,7 @@
 ACQ = 6
 OWN = 12
 QUARTERS, TILES, QUARTER = 4, 5, 640
+FIRST, SECOND = (0, 1), (2, 3)
 RUN = 8
 TOP, MID, RIM = 3, 5, 2
 
@@ -149,27 +150,36 @@
     def oth_rim(q):
         return rim_copy(1, q, core, oth, 2 * down, az_next)
 
-    def wait_rims():
-        for q in range(QUARTERS):
+    def start_rims(quarters):
+        @pl.when(has_down)
+        def _():
+            for q in quarters:
+                own_rim(q).start()
+                oth_rim(q).start()
+
+        @pl.when(jnp.logical_not(has_down))
+        def _():
+            for q in quarters:
+                own_rim(q).start()
+
+    def wait_rims(quarters):
+        for q in quarters:
             own_rim(q).wait_send()
 
         @pl.when(has_down)
         def _():
-            for q in range(QUARTERS):
+            for q in quarters:
                 oth_rim(q).wait_send()
 
     pl.semaphore_wait(barrier, expected)
 
-    @pl.when(both(has_next, has_down))
-    def _():
-        for q in range(QUARTERS):
-            own_rim(q).start()
-            oth_rim(q).start()
-
-    @pl.when(both(has_next, jnp.logical_not(has_down)))
-    def _():
-        for q in range(QUARTERS):
-            own_rim(q).start()
+    @pl.when(has_next)
+    def _():
+        start_rims(FIRST)
+
+    @pl.when(has_next)
+    def _():
+        start_rims(SECOND)
 
     @pl.when(core == 0)
     def _():
@@ -181,18 +191,12 @@
 
     @pl.when(has_up)
     def _():
-        for q in range(QUARTERS):
+        for q in FIRST:
             to_up(q).start()
 
-    rim_first = both(has_next, az % RUN == RUN - 1)
-
-    @pl.when(rim_first)
-    def _():
-        wait_rims()
-
     @pl.when(has_down)
     def _():
-        for q in range(QUARTERS):
+        for q in FIRST:
             to_down(q).start()
 
     loads[0].wait()
@@ -300,7 +304,23 @@
             place(q, t, left, jnp.concatenate([data(ownf, q, t, RIM, 5), nothing], axis=0))
         return carry
 
-    lax.fori_loop(0, QUARTERS, own_quarter, 0)
+    lax.fori_loop(0, 2, own_quarter, 0)
+
+    lax.fori_loop(2, QUARTERS, own_quarter, 0)
+
+    @pl.when(has_up)
+    def _():
+        for q in FIRST:
+            to_up(q).wait_send()
+        for q in SECOND:
+            to_up(q).start()
+
+    @pl.when(has_down)
+    def _():
+        for q in FIRST:
+            to_down(q).wait_send()
+        for q in SECOND:
+            to_down(q).start()
 
     loads[2].wait()
     loads[3].wait()
@@ -342,23 +362,29 @@
             turn[s, a, 1] = w * (sin_a * cos_b - cos_a * sin_b)
             turn[s, a, 2] = jnp.broadcast_to(w, (16, 128))
 
-    def rim_part(q):
+    def rim_part(h):
+        pair = (2 * h, 2 * h + 1)
+
         @pl.when(core == 0)
         def _():
-            for b in range(2):
-                rim_copy(0, q, b, own, me, az).wait_recv()
+            for q in pair:
+                for b in range(2):
+                    rim_copy(0, q, b, own, me, az).wait_recv()
 
         @pl.when(both(core == 0, has_up))
         def _():
-            for b in range(2):
-                rim_copy(1, q, b, oth, me, az).wait_recv()
-
-        lay(own, ownf, q, 0, RIM)
-        lay(oth, othf, q, 0, RIM)
-        for t in range(TILES):
-            right = jnp.concatenate([data(ownf, q, t, 0, RIM), data(othf, q, t, 0, RIM)], axis=0)
-            place(q, t, expand(q, t, 0, RIM), right)
-            add_power(q, t, 0, RIM)
+            for q in pair:
+                for b in range(2):
+                    rim_copy(1, q, b, oth, me, az).wait_recv()
+
+        for q in pair:
+            lay(own, ownf, q, 0, RIM)
+            lay(oth, othf, q, 0, RIM)
+        for q in pair:
+            for t in range(TILES):
+                right = jnp.concatenate([data(ownf, q, t, 0, RIM), data(othf, q, t, 0, RIM)], axis=0)
+                place(q, t, expand(q, t, 0, RIM), right)
+                add_power(q, t, 0, RIM)
 
     def main_part(q):
         @pl.when(both(core == 0, has_up))
@@ -381,13 +407,13 @@
     has_first = jnp.logical_or(core == 1, has_prev)
 
     def step(i, carry):
-        half = i // QUARTERS
-        rim = jnp.where(core == 1, i % 2, jnp.where(rim_late, half, 1 - half))
-        q = jnp.where(core == 1, i // 2, i % QUARTERS)
+        rim = jnp.where(core == 1, i % 3 // 2, jnp.where(rim_late, i // 4, 1 - jnp.minimum(i // 2, 1)))
+        h = jnp.where(core == 1, i // 3, i % 2)
+        q = jnp.where(core == 1, i - i // 3, jnp.where(rim_late, i, i - 2))
 
         @pl.when(both(rim == 1, has_first))
         def _():
-            rim_part(q)
+            rim_part(h)
 
         @pl.when(rim == 0)
         def _():
@@ -395,7 +421,7 @@
 
         return carry
 
-    lax.fori_loop(0, 2 * QUARTERS, step, 0)
+    lax.fori_loop(0, QUARTERS + 2, step, 0)
 
     for p in range(OWN // 2):
         turned[2 * p : 2 * p + 2] = jnp.transpose(acc[p].reshape(128, 128)).reshape(2, 64, 128)
@@ -446,12 +472,12 @@
 
     @pl.when(has_down)
     def _():
-        for q in range(QUARTERS):
+        for q in SECOND:
             to_down(q).wait_send()
 
     @pl.when(has_up)
     def _():
-        for q in range(QUARTERS):
+        for q in SECOND:
             to_up(q).wait_send()
 
         tab_up(core).wait_send()
@@ -464,9 +490,9 @@
     def _():
         to_core0.wait_send()
 
-    @pl.when(both(has_next, jnp.logical_not(rim_first)))
-    def _():
-        wait_rims()
+    @pl.when(has_next)
+    def _():
+        wait_rims(FIRST + SECOND)
 
     tab_chip.wait_send()
     fin_chip.wait_send()

time: 25.6 us -> 25.9 us (1.012)
  no operation moved by 1% of the time
where the time goes in v4:
time: 25.9 us; the launch traced here: 25.7 us
  Pallas kernels  23.7 us (92%)
  local copies, waits for them, and re-layouts  1.31 us (5%)
  between operations  0.64 us (2%)
    pallas_call x1, Pallas kernels, local(): pl.pallas_call(functools.partial(kernel, chips, slabs), out_shape=out, in...  23.7 us
    squeeze x1, local copies, waits for them, and re-layouts, local(): return (both[0], both[1])  1.31 us

profile of v4, /device:TPU:39, one launch (start us, length us, event | category | flops | bytes accessed | tf_op | source)
XLA Modules:
  0.0 25.7 jit_solution(5149806567691800511)
XLA Ops:
  0.6 23.7 %shard_map.59 = f32[2,6,2,128]{3,2,1,0:T(2,128)} custom-call(bf16[6,10,2,2560]{3,2,1,0:T(2,128)(2,1)} %bitcast.5, s32[6,10]{1,0:T(8,128)} %sec_hbm.1, s32[6]{0:T(128)} %cnt_hbm.1, f32[96,2,128]{2,1,0:T(2,128)} %screens_hbm.1), custom_call_target="tpu_custom_call" | custom-call | tf_op jit(solution)/shard_map/pallas_call | solution.py:527
  24.4 1.3 %slice_bitcast_fusion = (f32[6,2,128]{2,1,0:T(2,128)}, f32[6,2,128]{2,1,0:T(2,128)}) fusion(f32[2,6,2,128]{3,2,1,0:T(2,128)} %shard_map.59), kind=kLoop, calls=%fused_computation | loop fusion | bytes 24576 | tf_op jit(solution)/shard_map/squeeze | solution.py:574
